TPU v7x, 32 devices: a whole 2x2x4 slice. The times are simulated.
32 devices in a mesh: grp: 2 (over x), sub: 16 (over z, y, core).
Axes of the slice: x: 2, y: 2, z: 4, core: 2. Of those that a mesh axis runs over, the one named last changes fastest.
Arguments:
- schur_t: bfloat16 [2, 16, 1024, 1024], P('grp', 'sub')
- neumann_t: bfloat16 [2, 16, 1024, 1024], P('grp', 'sub')
- face_weights: float32 [2, 16, 1024], P('grp', 'sub'), as said below
- coarse_basis: bfloat16 [2, 16, 1024, 24], P('grp', 'sub'), may hold values from -0.375 to 0.375
- coarse_inverse: float32 [2, 192, 192], P('grp', 'sub')
- coarse_number: int32 [2, 384], P('grp'), may hold values from 0 to 191, as said below
- loads: bfloat16 [2, 16, 1024, 128], P('grp', 'sub'), may hold values from -6 to 6
- iterate: bfloat16 [2, 16, 1024, 128], P('grp', 'sub'), as said below
Outputs:
- iterate_out: bfloat16 [2, 16, 1024, 128], P('grp', 'sub')
Inputs may be any that keep to these rules, and one draw needn't show every extreme that they name: `face_weights`: the weights of an unknown and of its partner unknown on the face it shares sum to one. `coarse_number`: each value appears exactly twice in each group's row. `iterate`: equal on the two copies of each shared unknown.
All inputs are finite; a program needn't handle non-finite values.
Results may differ from a plain program's by a relative error of at most 0.0051.
Values sent between devices are 32-bit elements; how exact they have to be, the bound alone decides.
No kernel may reach another device: no remote copies, remote signals or barrier semaphores. Data moves between devices by JAX's collectives and lax.ppermute only.
A program may use at most 64 MiB of HBM per device.

v0:
```python
import functools

import jax
import jax.numpy as jnp
from jax import lax
from jax.experimental import pallas as pl
from jax.experimental.pallas import tpu as pltpu
from jax.sharding import PartitionSpec as P

ITERS = 3
HIGHEST = lax.Precision.HIGHEST
EVEN, ODD, BOTH = range(3)
LANES = 128
PIECES = 8
WEIGHT = 4 * 10**9
MIB = 2**20
WHOLE = pl.BlockSpec(memory_space=pltpu.VMEM)
AWAY = pl.BlockSpec(memory_space=pltpu.HBM)
ANYWHERE = pl.BlockSpec(memory_space=pl.ANY)


def channels(grp, sub, face):
    found = []
    for axis, devices, base in (("grp", grp, 2 * face), ("sub", sub, 0)):
        if devices == 2:
            found.append((axis, BOTH, base, 2 * face))
        else:
            found += [(axis, ODD, base, face), (axis, EVEN, base, face)]
    return tuple(found)


def mate(kind, index, devices):
    if kind == BOTH:
        return 1 - index
    step = 1 - 2 * (index % 2)
    if kind == ODD:
        step = -step
    return (index + step + devices) % devices


def swap(array, channel):
    axis, kind = channel[:2]
    devices = lax.axis_size(axis)
    return lax.ppermute(array, axis, [(i, mate(kind, i, devices)) for i in range(devices)])


def exchange(chans, sends):
    return tuple(swap(send, channel) for channel, send in zip(chans, sends))


def first_row(channel):
    axis, kind, base, rows = channel
    if kind == BOTH:
        return base
    odd = lax.rem(lax.axis_index(axis), 2)
    return pl.multiple_of(base + (odd if kind == ODD else 1 - odd) * rows, rows)


def own_rows(channel):
    return pl.ds(first_row(channel), channel[3])


def row_blocks(channel):
    blocks = channel[3] // LANES
    for block in range(blocks):
        rows = pl.ds(pl.multiple_of(first_row(channel) + block * LANES, LANES), LANES)
        yield block, rows, (block + blocks // 2) % blocks if channel[1] == BOTH else block


def across(channel, got):
    rows = channel[3]
    if channel[1] == BOTH:
        return jnp.concatenate([got[rows // 2 : rows], got[0 : rows // 2]], axis=0)
    return got[0:rows]


def product(a, b):
    return jnp.dot(a, b, preferred_element_type=jnp.float32)


def split(values, axis):
    high = values.astype(jnp.bfloat16)
    low = (values - high.astype(jnp.float32)).astype(jnp.bfloat16)
    return jnp.concatenate([high, low, high], axis=axis)


def thrice(values):
    high = values.astype(jnp.bfloat16).astype(jnp.float32)
    return jnp.concatenate([high, high, values - high], axis=1).astype(jnp.bfloat16)


def call(body, outs, args, scratch=(), flops=0, away=0, after=(), grant=16 * MIB, out=WHOLE):
    moved = sum(a.size * a.dtype.itemsize for a in args)
    ahead = len(after)
    return pl.pallas_call(
        lambda *refs: body(*refs[ahead:]),
        out_shape=outs,
        in_specs=[ANYWHERE] * ahead + [AWAY] * away + [WHOLE] * (len(args) - away),
        out_specs=jax.tree.map(lambda _: out, outs),
        scratch_shapes=scratch,
        cost_estimate=pl.CostEstimate(flops=flops, bytes_accessed=moved, transcendentals=0),
        compiler_params=pltpu.CompilerParams(vmem_limit_bytes=grant),
    )(*after, *args)


class Values:
    def __init__(self, chans, ncl, near, far, second):
        self.chans, self.ncl = chans, ncl
        self.near, self.far, self.second = near, far, second
        self.order = near_order(chans)

    def at(self, *path):
        grp = [c for c in path if self.chans[c][0] == "grp"]
        sub = [c for c in path if self.chans[c][0] == "sub"]
        grp, sub = [[] if len(p) == 2 and p[0] == p[1] else p for p in (grp, sub)]
        if len(grp) == 2:
            return self.second[grp[0]][...]
        source = self.far[grp[0]] if grp else self.near
        place = self.order.index(tuple(sub)) * self.ncl
        return source[place : place + self.ncl]

    def around(self, *path):
        return [self.at(*path)] + [self.at(*path, c) for c in range(len(self.chans))]


def near_order(chans):
    kinds = [c for c, channel in enumerate(chans) if channel[0] == "sub"]
    return [()] + [(c,) for c in kinds] + [(c, d) for c in kinds for d in kinds if c != d]


def value_refs(chans, ncl, refs):
    far = sum(channel[0] == "grp" for channel in chans)
    second = far if far > 1 else 0
    values = Values(chans, ncl, refs[0], refs[1 : 1 + far], refs[1 + far : 1 + far + second])
    return values, refs[1 + far + second :]


def opening(chans, matrix, load, state, basis_across, *refs):
    count = len(refs) // 2 - 2
    outs, (rows, mine, now, basis, sems), sends = refs[:count], refs[count : count + 5], refs[count + 5 :]
    piece = matrix.shape[0] // PIECES
    order = [(at + PIECES // 2) % PIECES * piece for at in range(PIECES)]
    pairs = [(state, now), (load, mine), (basis_across, basis)]
    pairs += [(matrix.at[pl.ds(at, piece)], rows.at[pl.ds(at, piece)]) for at in order]
    copies = [pltpu.make_async_copy(a, b, sems.at[i]) for i, (a, b) in enumerate(pairs)]
    for copy in copies:
        copy.start()
    first = 3 + PIECES // 2
    for copy in copies[:first]:
        copy.wait()
    waiting = copies[first:]
    written = []

    def write(send):
        at = len(written)
        written.append(pltpu.make_async_copy(send, outs[at], sems.at[len(pairs) + at]))
        written[-1].start()

    for channel, send in zip(chans, sends):
        if channel[0] == "sub":
            while waiting:
                waiting.pop(0).wait()
        own = own_rows(channel)
        send[0 : channel[3]] = mine[own].astype(jnp.float32) - product(rows[own], now[...])
        if channel[0] == "sub":
            basis_on(channel, basis, send, channel[3])
        write(send)
    for channel, send in zip(chans, sends[len(chans) :]):
        basis_on(channel, basis, send, 0)
        write(send)
    for copy in written:
        copy.wait()


def basis_on(channel, basis, send, start):
    ncl = basis.shape[0]
    for block, columns, _ in row_blocks(channel):
        at = start + block * ncl
        send[at : at + ncl] = basis[:, columns].astype(jnp.float32)


def smooth(chans, weights, resid_on, weighted):
    for at, channel in enumerate(chans):
        own = own_rows(channel)
        weighted[own] = (weights[own] * resid_on(at, own)).astype(jnp.bfloat16)


def smoothing_near(chans, matrix, weights, weighted, sends):
    for channel, send in zip(chans, sends):
        own = own_rows(channel)
        send[...] = weights[own] * product(matrix[own], weighted[...])


def stash(*refs):
    count = len(refs) // 2
    for part, out in zip(refs[:count], refs[count:]):
        out[...] = part[0 : out.shape[0]]


def summing(chans, *refs):
    count = len(chans)
    parts, gots, out = refs[:count], refs[count : 2 * count], refs[2 * count]
    for channel, part, got in zip(chans, parts, gots):
        out[own_rows(channel)] = part[0 : channel[3]] + across(channel, got)


def smoothing_first(chans, far, matrix, weights, *refs):
    count = len(chans)
    parts, gots = refs[:count], refs[count : 2 * count]

    def resid_on(at, own):
        return parts[at][...] + across(chans[at], gots[at])

    smooth(chans, weights, resid_on, refs[2 * count])
    smoothing_near(far, matrix, weights, refs[2 * count], refs[2 * count + 1 :])


def correct(chans, ncl, weights, ahead, spread, summed, refs):
    reach = refs[: len(chans)]
    values, refs = value_refs(chans, ncl, refs[len(chans) :])
    state, weighted, rest = refs[0], refs[1], refs[2:]
    here = values.around()

    def resid_on(at, own):
        pair = jnp.concatenate([here[0], values.at(at)], axis=0)
        state[own] = (ahead[own] + product(spread[own], split(pair, 0))).astype(state.dtype)
        both = jnp.concatenate(here + values.around(at), axis=0)
        return summed[own] - product(reach[at][...], split(both, 0)[0 : 2 * both.shape[0]])

    smooth(chans, weights, resid_on, weighted)
    return weighted, rest


def smoothing_far(chans, far, ncl, matrix, weights, ahead, spread, summed, *refs):
    weighted, sends = correct(chans, ncl, weights, ahead, spread, summed, refs)
    smoothing_near(far, matrix, weights, weighted, sends)


def smoothing_last(chans, ncl, basis_across, weights, ahead, spread, summed, *refs):
    weighted, (coarse,) = correct(chans, ncl, weights, ahead, spread, summed, refs)
    coarse[...] = product(basis_across[...], weighted[...])


def smoothing_rows(chans, matrix, weights, weighted, *sends):
    smoothing_near(chans, matrix, weights, weighted, sends)


def smoothing_sub(near, matrix, weights, weighted, basis_across, *refs):
    inverse = refs[: -len(near) - 1]
    coarse, sends = refs[-len(near) - 1], refs[-len(near) :]
    ncl = basis_across.shape[0]
    coarse[0:ncl] = product(basis_across[...], weighted[...])
    for rows in inverse:
        padded = rows.shape[0] + -rows.shape[0] % 8
        coarse[ncl:] = jnp.zeros((coarse.shape[0] - ncl, coarse.shape[1]), jnp.float32)
        for at in range(0, rows.shape[1], LANES):
            start = ncl + at // LANES * padded
            columns = min(LANES, rows.shape[1] - at)
            coarse[start : start + rows.shape[0], 0:columns] = rows[:, at : at + columns]
    smoothing_near(near, matrix, weights, weighted, sends)


def spreading(chans, weights, basis_across, *refs):
    gots, thin, full = refs[:-2], refs[-2], refs[-1]
    ncl = basis_across.shape[0]
    width = full.shape[1] // 2
    for at, (channel, got) in enumerate(zip(chans, gots)):
        for _, own, block in row_blocks(channel):
            from_row = block * ncl + (channel[3] if channel[0] == "sub" else 0)
            weight = weights[own][:, 0:ncl]
            here = weight * basis_across[:, own].astype(jnp.float32).T
            there = (1.0 - weight) * got[from_row : from_row + ncl].T
            thin[own] = thrice(jnp.concatenate([here, there], axis=1))
            before = [jnp.zeros((LANES, at * ncl), jnp.float32)] if at else []
            behind = jnp.zeros((LANES, width - (at + 2) * ncl), jnp.float32)
            placed = jnp.concatenate([here, *before, there, behind], axis=1)
            high = placed.astype(jnp.bfloat16)
            full[own, 0:width] = high
            full[own, width:] = (placed - high.astype(jnp.float32)).astype(jnp.bfloat16)


def responding(matrix, full, out, turned):
    width = out.shape[1]
    both = product(matrix[...], full[...])
    out[...] = both[:, 0:width] + both[:, width:]
    for at in range(0, out.shape[0], LANES):
        turned[:, at : at + LANES] = out[at : at + LANES].T


def reaching(channel, count, response, got, out):
    for block, own, from_block in row_blocks(channel):
        at = channel[3] + from_block * count
        theirs = got[at : at + count].T
        both = jnp.concatenate([response[own][:, 0:count], theirs], axis=1)
        out[block * LANES : (block + 1) * LANES] = jnp.concatenate([both, both], axis=1).astype(jnp.bfloat16)


def joining(first, second, out):
    out[...] = jnp.concatenate([first[...], second[...]], axis=0)


def coarse_first(chans, order, sub, ncl, numbers, kept, got, out, values, *scratch):
    arranged, upright, relative, pieces = scratch
    index = lax.axis_index("sub")
    rows_of = order // sub
    padded = rows_of + -rows_of % 8
    stride = kept.shape[0] * 2 // sub
    upright[...] = jnp.broadcast_to(numbers[...].astype(jnp.float32), (8, numbers.shape[1])).T
    for block, origin in enumerate(origins(sub)):
        origin = jnp.bitwise_xor(index, origin)
        half = sub // 2
        source = kept if block < half else got
        at = (block % half) * stride
        pieces[block * ncl : (block + 1) * ncl] = source[at : at + ncl]
        to = pl.ds(pl.multiple_of(origin * padded, 8), padded)
        for tile in range(arranged.shape[1] // LANES):
            start = at + ncl + tile * padded
            arranged[to, tile * LANES : (tile + 1) * LANES] = source[start : start + padded]
        relative[block * ncl : (block + 1) * ncl] = upright[pl.ds(pl.multiple_of(origin * ncl, 8), ncl)]
    wanted = []
    for path in near_order(chans):
        place = index
        for c in path:
            place = mate(chans[c][1], place, sub)
        wanted.append(upright[pl.ds(pl.multiple_of(place * ncl, 8), ncl)])
    wanted = jnp.concatenate(wanted, axis=0)[:, 0:1].astype(jnp.int32)
    lane = lax.broadcasted_iota(jnp.int32, (wanted.shape[0], sub * padded), 1)
    inside = lane % padded
    held = jnp.where(inside < rows_of, (lane // padded) * rows_of + inside, -1)
    pick = jnp.where(wanted == held, 1.0, 0.0).astype(jnp.float32)
    chosen = jnp.dot(pick, arranged[...], precision=HIGHEST, preferred_element_type=jnp.float32)
    column = lax.broadcasted_iota(jnp.int32, (relative.shape[0], arranged.shape[1]), 1)
    place = jnp.where(relative[...][:, 0:1].astype(jnp.int32) == column, 1.0, 0.0).astype(jnp.float32)
    whole = lax.dot_general(
        chosen, place, (((1,), (1,)), ((), ())), precision=HIGHEST, preferred_element_type=jnp.float32
    )
    values[...] = jnp.dot(whole, pieces[...], precision=HIGHEST, preferred_element_type=jnp.float32)
    half = whole.shape[1] // 2
    out[:, 0 : 3 * half] = thrice(whole[:, 0:half])
    out[:, 3 * half :] = thrice(whole[:, half:])


def coarse_values(mapping, kept, got, out):
    half = mapping.shape[1] // 2
    out[...] = product(mapping[:, 0:half], split(kept[...], 0)) + product(mapping[:, half:], split(got[...], 0))


def between_far(chans, far, count, matrix, load, state, *refs):
    size = len(chans)
    parts, gots = refs[:size], refs[size : 2 * size]
    turned = refs[2 * size : -len(far) - 2]
    ahead, rounded, sends = refs[-len(far) - 2], refs[-len(far) - 1], refs[-len(far) :]
    for channel, part, got in zip(chans, parts, gots):
        own = own_rows(channel)
        ahead[own] = state[own].astype(jnp.float32) + part[...] + across(channel, got)
        rounded[own] = ahead[own].astype(rounded.dtype)
    between_near(far, count, matrix, load, rounded, *turned, *sends)


def between_near(chans, count, matrix, load, state, *refs):
    sends = refs[-len(chans) :]
    for channel, send in zip(chans, sends):
        rows = channel[3]
        own = own_rows(channel)
        send[0:rows] = load[own].astype(jnp.float32) - product(matrix[own], state[...])
        for turned in refs[: -len(chans)]:
            for block, columns, _ in row_blocks(channel):
                send[rows + block * count : rows + (block + 1) * count] = turned[0:count, columns]


def landing(chans, ncl, state, spread, near_values, *refs):
    count = len(chans)
    parts, gots, out = refs[:count], refs[count : 2 * count], refs[2 * count]
    values = Values(chans, ncl, near_values, (), ())
    for at, channel in enumerate(chans):
        own = own_rows(channel)
        theirs = values.at(at) if channel[0] == "sub" else jnp.zeros((ncl, state.shape[1]), jnp.float32)
        update = product(spread[own], split(jnp.concatenate([values.at(), theirs], axis=0), 0))
        update += parts[at][...] + across(channel, gots[at])
        out[own] = state[own].astype(jnp.float32) + update


def closing(chans, ncl, spread, landed, *refs):
    values, (out, rounded, sems) = value_refs(chans, ncl, refs)
    half = rounded.shape[0] // 2
    copies = [
        pltpu.make_async_copy(rounded.at[pl.ds(at, half)], out.at[pl.ds(at, half)], sems.at[i])
        for i, at in enumerate((0, half))
    ]
    rounded[0:half] = landed[0:half].astype(rounded.dtype)
    copies[0].start()
    for at, channel in enumerate(chans):
        if channel[0] == "grp":
            own = own_rows(channel)
            theirs = values.at(at)
            pair = jnp.concatenate([jnp.zeros_like(theirs), theirs], axis=0)
            rounded[own] = (landed[own] + product(spread[own], split(pair, 0))).astype(rounded.dtype)
    copies[1].start()
    for copy in copies:
        copy.wait()


def steps(sub):
    found, step = [], sub // 2
    while step:
        found.append(step)
        step //= 2
    return found


def origins(sub):
    found = [0]
    for step in steps(sub):
        found += [origin ^ step for origin in found]
    return found


def gathered(piece, sub, hold=(), wide=False, early=()):
    def hop(move):
        return lax.ppermute(piece, "sub", [(i, i ^ move) for i in range(sub)])

    moves = steps(sub)
    if wide:
        first, second, *moves = moves
        pieces = [piece] + [hop(move) for move in (first, second, first ^ second)]
        piece = jnp.concatenate(pieces, axis=0)
    for at, move in enumerate(moves[:-1]):
        got = hop(move)
        after = hold if at + 1 == len(moves) // 2 else early if at == 0 else ()
        if after:
            joined = jax.ShapeDtypeStruct((2 * piece.shape[0], piece.shape[1]), piece.dtype)
            piece = call(joining, joined, (piece, got), after=after, flops=0 if after is hold else WEIGHT // 2)
        else:
            piece = jnp.concatenate([piece, got], axis=0)
    return piece, hop(moves[-1])


def shards(
    schur_t, neumann_t, face_weights, coarse_basis, coarse_inverse, coarse_number, loads, iterate
):
    schur, neumann = schur_t[0, 0], neumann_t[0, 0]
    basis_across = coarse_basis[0, 0].T
    load, state = loads[0, 0], iterate[0, 0]
    iface, columns = state.shape
    ncl = basis_across.shape[0]
    face = iface // 4
    grp, sub = lax.axis_size("grp"), lax.axis_size("sub")
    chans = channels(grp, sub, face)
    far = tuple(c for c in chans if c[0] == "grp")
    near = chans[len(far) :]
    around = (len(chans) + 1) * ncl
    order = coarse_inverse.shape[2]

    def wide(rows, width=columns):
        return jax.ShapeDtypeStruct((rows, width), jnp.float32)

    def short(rows, width=columns):
        return jax.ShapeDtypeStruct((rows, width), jnp.bfloat16)

    far_plain, near_plain = [tuple(wide(c[3]) for c in group) for group in (far, near)]
    half = short(iface)
    flops = iface * iface * columns

    opened = (
        *far_plain,
        *(wide(c[3] + c[3] // LANES * ncl) for c in near),
        *(wide(c[3] // LANES * ncl) for c in far),
    )
    parts = call(
        functools.partial(opening, chans),
        opened,
        (schur, load, state, basis_across),
        scratch=(
            pltpu.VMEM(schur.shape, schur.dtype),
            pltpu.VMEM(load.shape, load.dtype),
            pltpu.VMEM(state.shape, state.dtype),
            pltpu.VMEM(basis_across.shape, basis_across.dtype),
            pltpu.SemaphoreType.DMA((3 + PIECES + len(opened),)),
            *(pltpu.VMEM(out.shape, out.dtype) for out in opened),
        ),
        flops=2 * flops,
        away=4,
        grant=56 * MIB,
        out=AWAY,
    )
    parts, far_basis = parts[: len(chans)], parts[len(chans) :]
    gots = exchange(chans, parts)
    basis_gots = (*exchange(far, far_basis), *gots[len(far) :])
    parts = call(stash, far_plain + near_plain, tuple(parts))

    weights = jnp.broadcast_to(face_weights[0, 0][:, None], (iface, columns))
    rows_of = coarse_inverse.shape[1]
    tiles = (order + -order % LANES) // LANES
    inverse_rows = (rows_of + -rows_of % 8) * tiles
    mapping = None

    def coarse_step(coarse, mapping, hold=(), after=(), early=(), sent=1 + len(near)):
        rows = len(near_order(chans)) * ncl
        kept, got = gathered(coarse, sub, hold, False, early)
        if mapping is None:
            mapping, own = call(
                functools.partial(coarse_first, chans, order, sub, ncl),
                (short(rows, 3 * sub * ncl), wide(rows)),
                (coarse_number, kept, got),
                scratch=(
                    pltpu.VMEM((inverse_rows // tiles * sub, tiles * LANES), jnp.float32),
                    pltpu.VMEM((sub * ncl, 8), jnp.float32),
                    pltpu.VMEM((sub * ncl, 8), jnp.float32),
                    pltpu.VMEM((sub * ncl, columns), jnp.float32),
                ),
                after=after,
            )
        else:
            own = call(coarse_values, wide(rows), (mapping, kept, got), after=after)
        known = own[0 : sent * ncl]
        theirs = [swap(known, channel) for channel in far]
        beyond = []
        if len(far) > 1:
            beyond = [swap(theirs[1 - at][0:ncl], channel) for at, channel in enumerate(far)]
        return mapping, (own, *theirs, *beyond)

    def sums(sent, got):
        return call(functools.partial(summing, chans), wide(iface), (*sent, *got), flops=WEIGHT)

    for step in range(ITERS):
        start, last = step == 0, step + 1 == ITERS
        if start:
            weighted, *far_scaled = call(
                functools.partial(smoothing_first, chans, far),
                (half,) + far_plain,
                (neumann, weights, *parts, *gots),
                flops=flops,
            )
        else:
            early = (response,) if step == 1 else near_scaled[:1]
            mapping, values = coarse_step(coarse, mapping, hold=far_parts[:1], early=early)
            if step == 1:
                reach = [
                    call(
                        functools.partial(reaching, channel, around),
                        short(channel[3], 4 * around),
                        (response, got),
                        after=values[:1],
                    )
                    for channel, got in zip(chans, gots)
                ]
            known = (weights, ahead, spread, sums(parts, gots), *reach, *values)
            if last:
                state, weighted, coarse = call(
                    functools.partial(smoothing_last, chans, ncl),
                    (half, half, wide(ncl)),
                    (basis_across, *known),
                )
                far_scaled = call(
                    functools.partial(smoothing_rows, far),
                    far_plain,
                    (neumann, weights, weighted),
                    flops=flops,
                )
                near_scaled = call(
                    functools.partial(smoothing_rows, near),
                    near_plain,
                    (neumann, weights, weighted),
                    flops=flops,
                    after=far_scaled[:1],
                )
            else:
                state, weighted, *far_scaled = call(
                    functools.partial(smoothing_far, chans, far, ncl),
                    (half, half) + far_plain,
                    (neumann, *known),
                    flops=flops,
                )
        if not last:
            inverse = (coarse_inverse[0],) if start else ()
            coarse, *near_scaled = call(
                functools.partial(smoothing_sub, near),
                (wide(ncl + len(inverse) * inverse_rows),) + near_plain,
                (neumann, weights, weighted, basis_across, *inverse),
                flops=flops,
            )
        scaled = (*far_scaled, *near_scaled)
        scaled_gots = exchange(chans, scaled)
        behind, behind_rows = (), 0
        if start:
            width = around + -around % LANES
            spread, full = call(
                functools.partial(spreading, chans),
                (short(iface, 6 * ncl), short(iface, 2 * width)),
                (weights, basis_across, *basis_gots),
                after=near_scaled[:1],
            )
            response, turned = call(
                responding, (wide(iface, width), wide(width, iface)), (schur, full), flops=2 * flops
            )
            behind, behind_rows = (turned,), around
        if not last:
            far_outs, near_outs = [
                tuple(wide(c[3] + c[3] // LANES * behind_rows) for c in group) for group in (far, near)
            ]
            ahead, rounded, *far_parts = call(
                functools.partial(between_far, chans, far, around),
                (wide(iface), half) + far_outs,
                (schur, load, state, *scaled, *scaled_gots, *behind),
                flops=flops,
            )
            near_parts = call(
                functools.partial(between_near, near, around),
                near_outs,
                (schur, load, rounded, *behind),
                flops=flops,
                after=far_parts[:1],
            )
            parts = (*far_parts, *near_parts)
            gots = exchange(chans, parts)
    mapping, values = coarse_step(coarse, mapping, after=scaled_gots[len(far) :], sent=1)
    landed = call(
        functools.partial(landing, chans, ncl),
        wide(iface),
        (state, spread, values[0], *scaled, *scaled_gots),
        flops=WEIGHT,
    )
    out = call(
        functools.partial(closing, chans, ncl),
        half,
        (spread, landed, *values),
        scratch=(pltpu.VMEM(half.shape, half.dtype), pltpu.SemaphoreType.DMA((2,))),
        out=AWAY,
    )
    return out[None, None]


def solution(mesh):
    return jax.shard_map(
        shards,
        mesh=mesh,
        in_specs=(
            P("grp", "sub", None, None),
            P("grp", "sub", None, None),
            P("grp", "sub", None),
            P("grp", "sub", None, None),
            P("grp", "sub", None),
            P("grp", None),
            P("grp", "sub", None, None),
            P("grp", "sub", None, None),
        ),
        out_specs=P("grp", "sub", None, None),
        check_vma=False,
    )
```

profile of v0, /device:TPU:0, one launch (start us, length us, event | category | flops | bytes accessed | tf_op | source)
XLA Modules:
  0.0 83.3 jit_solution(1388396517316679431)
XLA Ops:
  0.0 3.7 %shard_map.82 = (f32[512,128]{1,0:T(8,128)}, f32[304,128]{1,0:T(8,128)}, f32[304,128]{1,0:T(8,128)}, f32[96,128]{1,0:T(8,128)}) custom-call(bf16[1024,1024]{1,0:T(8,128)(2,1)} %bitcast.12, bf16[1024,128]{1,0:T(8,128)(2,1)} %bitcast.24, bf16[1024,128]{1,0:T(8,128)(2,1)} %bitcast.34, bf16[24,1024]{1,0:T(8,128)(2,1)} %bitcast.29), custom_call_target="tpu_custom_call" | custom-call | flops 268435456 | bytes 2670592 | tf_op jit(solution)/shard_map/pallas_call | solution.py:95
  3.7 3.0 %collective-permute-start = (f32[512,128]{1,0:T(8,128)}, f32[512,128]{1,0:T(8,128)S(1)}, u32[]{:S(2)}, u32[]{:S(2)}) collective-permute-start(f32[512,128]{1,0:T(8,128)} %get-tuple-element.44.refs_0_), channel_id=1, source_target_pairs={{0,16},{16,0},{1,17},{17,1},{2,18},{18,2},{3,19},{19,3},{4,20},{20... | collective-permute-start | bytes 786440 | tf_op jit(solution)/shard_map/ppermute | solution.py:44
  6.7 3.7 %collective-permute-start.1 = (f32[304,128]{1,0:T(8,128)}, f32[304,128]{1,0:T(8,128)S(1)}, u32[]{:S(2)}, u32[]{:S(2)}) collective-permute-start(f32[304,128]{1,0:T(8,128)} %get-tuple-element.45.refs_1_), channel_id=1, source_target_pairs={{0,15},{1,2},{2,1},{3,4},{4,3},{5,6},{6,5},{7,8},{8,7},{9,10},{10,... | collective-permute-start | bytes 466952 | tf_op jit(solution)/shard_map/ppermute | solution.py:44
  16.8 2.7 %collective-permute-start.10 = (f32[56,128]{1,0:T(8,128)S(1)}, f32[56,128]{1,0:T(8,128)S(1)}, u32[]{:S(2)}, u32[]{:S(2)}) collective-permute-start(f32[56,128]{1,0:T(8,128)S(1)} %get-tuple-element.64.refs_1_), channel_id=1, source_target_pairs={{0,8},{1,9},{2,10},{3,11},{4,12},{5,13},{6,14},{7,15},{8,0},{9,1},... | collective-permute-start | bytes 86024 | tf_op jit(solution)/shard_map/ppermute | solution.py:420
  19.7 1.4 %collective-permute-start.6 = (f32[256,128]{1,0:T(8,128)S(1)}, f32[256,128]{1,0:T(8,128)S(1)}, u32[]{:S(2)}, u32[]{:S(2)}) collective-permute-start(f32[256,128]{1,0:T(8,128)S(1)} %get-tuple-element.55.refs_5_), channel_id=1, source_target_pairs={{0,1},{1,0},{2,3},{3,2},{4,5},{5,4},{6,7},{7,6},{8,9},{9,8},{10,11... | collective-permute-start | bytes 393224 | tf_op jit(solution)/shard_map/ppermute | solution.py:44
  23.1 1.6 %collective-permute-start.11 = (f32[112,128]{1,0:T(8,128)S(1)}, f32[112,128]{1,0:T(8,128)S(1)}, u32[]{:S(2)}, u32[]{:S(2)}) collective-permute-start(f32[112,128]{1,0:T(8,128)S(1)} %shard_map.91.refs_1_), channel_id=1, source_target_pairs={{0,4},{1,5},{2,6},{3,7},{4,0},{5,1},{6,2},{7,3},{8,12},{9,13},{10,... | collective-permute-start | bytes 172040 | tf_op jit(solution)/shard_map/ppermute | solution.py:420
  24.8 1.8 %collective-permute-done.5.refs_7_ = f32[256,128]{1,0:T(8,128)S(1)} collective-permute-done((f32[256,128]{1,0:T(8,128)S(1)}, f32[256,128]{1,0:T(8,128)S(1)}, u32[]{:S(2)}, u32[]{:S(2)}) %collective-permute-start.5) | collective-permute-done | bytes 131104 | tf_op jit(solution)/shard_map/ppermute | solution.py:44
  27.4 1.6 %collective-permute-start.12 = (f32[224,128]{1,0:T(8,128)S(1)}, f32[224,128]{1,0:T(8,128)S(1)}, u32[]{:S(2)}, u32[]{:S(2)}) collective-permute-start(f32[224,128]{1,0:T(8,128)S(1)} %shard_map.92), channel_id=1, source_target_pairs={{0,2},{1,3},{2,0},{3,1},{4,6},{5,7},{6,4},{7,5},{8,10},{9,11},{10,... | collective-permute-start | bytes 344072 | tf_op jit(solution)/shard_map/ppermute | solution.py:420
  29.5 2.7 %collective-permute-done.12 = f32[224,128]{1,0:T(8,128)S(1)} collective-permute-done((f32[224,128]{1,0:T(8,128)S(1)}, f32[224,128]{1,0:T(8,128)S(1)}, u32[]{:S(2)}, u32[]{:S(2)}) %collective-permute-start.12) | collective-permute-done | bytes 114720 | tf_op jit(solution)/shard_map/ppermute | solution.py:420
  32.8 3.7 %collective-permute-start.8 = (f32[448,128]{1,0:T(8,128)S(1)}, f32[448,128]{1,0:T(8,128)S(1)}, u32[]{:S(2)}, u32[]{:S(2)}) collective-permute-start(f32[448,128]{1,0:T(8,128)S(1)} %get-tuple-element.61.refs_1_), channel_id=1, source_target_pairs={{0,15},{1,2},{2,1},{3,4},{4,3},{5,6},{6,5},{7,8},{8,7},{9,10},{10,... | collective-permute-start | bytes 688136 | tf_op jit(solution)/shard_map/ppermute | solution.py:44
  36.5 1.9 %shard_map.93 = (bf16[120,1152]{1,0:T(8,128)(2,1)S(1)}, f32[120,128]{1,0:T(8,128)S(1)}) custom-call(s32[1,384]{1,0:T(1,128)S(1)} %copy-done.8, f32[448,128]{1,0:T(8,128)S(1)} %pad_maximum_fusion.refs_1_, f32[448,128]{1,0:T(8,128)S(1)} %collective-permute-done.13.refs_2_), custom_call_target="tpu_custom_call" | custom-call | bytes 460288 | tf_op jit(solution)/shard_map/pallas_call | solution.py:95
  39.1 2.0 %collective-permute-done.8.refs_4_.refs_2_ = f32[448,128]{1,0:T(8,128)S(1)} collective-permute-done((f32[448,128]{1,0:T(8,128)S(1)}, f32[448,128]{1,0:T(8,128)S(1)}, u32[]{:S(2)}, u32[]{:S(2)}) %collective-permute-start.8) | collective-permute-done | bytes 229408 | tf_op jit(solution)/shard_map/ppermute | solution.py:44
  44.8 3.0 %collective-permute-start.16 = (f32[256,128]{1,0:T(8,128)S(1)}, f32[256,128]{1,0:T(8,128)S(1)}, u32[]{:S(2)}, u32[]{:S(2)}) collective-permute-start(f32[256,128]{1,0:T(8,128)S(1)} %get-tuple-element.69.refs_4_.refs_0_), channel_id=1, source_target_pairs={{0,15},{1,2},{2,1},{3,4},{4,3},{5,6},{6,5},{7,8},{8,7},{9,10},{10,... | collective-permute-start | bytes 393224 | tf_op jit(solution)/shard_map/ppermute | solution.py:44
  47.8 1.6 %collective-permute-done.21.refs_2_ = f32[24,128]{1,0:T(8,128)S(1)} collective-permute-done((f32[24,128]{1,0:T(8,128)S(1)}, f32[24,128]{1,0:T(8,128)S(1)}, u32[]{:S(2)}, u32[]{:S(2)}) %collective-permute-start.21) | collective-permute-done | bytes 12320 | tf_op jit(solution)/shard_map/ppermute | solution.py:420
  49.4 2.6 %collective-permute-done.16.refs_7_ = f32[256,128]{1,0:T(8,128)S(1)} collective-permute-done((f32[256,128]{1,0:T(8,128)S(1)}, f32[256,128]{1,0:T(8,128)S(1)}, u32[]{:S(2)}, u32[]{:S(2)}) %collective-permute-start.16) | collective-permute-done | bytes 131104 | tf_op jit(solution)/shard_map/ppermute | solution.py:44
  54.0 1.5 %collective-permute-start.18 = (f32[512,128]{1,0:T(8,128)S(1)}, f32[512,128]{1,0:T(8,128)S(1)}, u32[]{:S(2)}, u32[]{:S(2)}) collective-permute-start(f32[512,128]{1,0:T(8,128)S(1)} %get-tuple-element.72.refs_0_), channel_id=1, source_target_pairs={{0,16},{16,0},{1,17},{17,1},{2,18},{18,2},{3,19},{19,3},{4,20},{20... | collective-permute-start | bytes 786440 | tf_op jit(solution)/shard_map/ppermute | solution.py:44
  55.9 1.9 %collective-permute-start.19 = (f32[256,128]{1,0:T(8,128)S(1)}, f32[256,128]{1,0:T(8,128)S(1)}, u32[]{:S(2)}, u32[]{:S(2)}) collective-permute-start(f32[256,128]{1,0:T(8,128)S(1)} %get-tuple-element.74.refs_1_), channel_id=1, source_target_pairs={{0,15},{1,2},{2,1},{3,4},{4,3},{5,6},{6,5},{7,8},{8,7},{9,10},{10,... | collective-permute-start | bytes 393224 | tf_op jit(solution)/shard_map/ppermute | solution.py:44
  60.5 2.5 %collective-permute-done.19.refs_4_ = f32[256,128]{1,0:T(8,128)S(1)} collective-permute-done((f32[256,128]{1,0:T(8,128)S(1)}, f32[256,128]{1,0:T(8,128)S(1)}, u32[]{:S(2)}, u32[]{:S(2)}) %collective-permute-start.19) | collective-permute-done | bytes 131104 | tf_op jit(solution)/shard_map/ppermute | solution.py:44
  66.5 2.1 %collective-permute-start.26 = (f32[256,128]{1,0:T(8,128)S(1)}, f32[256,128]{1,0:T(8,128)S(1)}, u32[]{:S(2)}, u32[]{:S(2)}) collective-permute-start(f32[256,128]{1,0:T(8,128)S(1)} %get-tuple-element.80.refs_4_), channel_id=1, source_target_pairs={{0,15},{1,2},{2,1},{3,4},{4,3},{5,6},{6,5},{7,8},{8,7},{9,10},{10,... | collective-permute-start | bytes 393224 | tf_op jit(solution)/shard_map/ppermute | solution.py:44
  70.1 2.8 %collective-permute-done.29 = f32[48,128]{1,0:T(8,128)S(1)} collective-permute-done((f32[48,128]{1,0:T(8,128)S(1)}, f32[48,128]{1,0:T(8,128)S(1)}, u32[]{:S(2)}, u32[]{:S(2)}) %collective-permute-start.29) | collective-permute-done | bytes 24608 | tf_op jit(solution)/shard_map/ppermute | solution.py:420
  72.9 1.9 %collective-permute-start.30 = (f32[96,128]{1,0:T(8,128)S(1)}, f32[96,128]{1,0:T(8,128)S(1)}, u32[]{:S(2)}, u32[]{:S(2)}) collective-permute-start(f32[96,128]{1,0:T(8,128)S(1)} %pad_maximum_fusion.2), channel_id=1, source_target_pairs={{0,2},{1,3},{2,0},{3,1},{4,6},{5,7},{6,4},{7,5},{8,10},{9,11},{10,... | collective-permute-start | bytes 147464 | tf_op jit(solution)/shard_map/ppermute | solution.py:420
  74.8 2.2 %collective-permute-done.30 = f32[96,128]{1,0:T(8,128)S(1)} collective-permute-done((f32[96,128]{1,0:T(8,128)S(1)}, f32[96,128]{1,0:T(8,128)S(1)}, u32[]{:S(2)}, u32[]{:S(2)}) %collective-permute-start.30) | collective-permute-done | bytes 49184 | tf_op jit(solution)/shard_map/ppermute | solution.py:420
  77.0 1.3 %collective-permute-done.31.refs_4_ = f32[192,128]{1,0:T(8,128)S(1)} collective-permute-done((f32[192,128]{1,0:T(8,128)S(1)}, f32[192,128]{1,0:T(8,128)S(1)}, u32[]{:S(2)}, u32[]{:S(2)}) %collective-permute-start.31) | collective-permute-done | bytes 98336 | tf_op jit(solution)/shard_map/ppermute | solution.py:420
  80.0 2.3 %collective-permute-done.33.refs_3_ = f32[24,128]{1,0:T(8,128)S(1)} collective-permute-done((f32[24,128]{1,0:T(8,128)S(1)}, f32[24,128]{1,0:T(8,128)S(1)}, u32[]{:S(2)}, u32[]{:S(2)}) %collective-permute-start.33) | collective-permute-done | bytes 12320 | tf_op jit(solution)/shard_map/ppermute | solution.py:44
  (108 shorter events, 27.5 us)
Async XLA Ops:
  3.7 10.6 %collective-permute-start = (f32[512,128]{1,0:T(8,128)}, f32[512,128]{1,0:T(8,128)S(1)}, u32[]{:S(2)}, u32[]{:S(2)}) collective-permute-start(f32[512,128]{1,0:T(8,128)} %get-tuple-element.44.refs_0_), channel_id=1, source_target_pairs={{0,16},{16,0},{1,17},{17,1},{2,18},{18,2},{3,19},{19,3},{4,20},{20... | collective-permute-start | bytes 786440 | tf_op jit(solution)/shard_map/ppermute | solution.py:44
  6.7 7.6 %collective-permute-start.1 = (f32[304,128]{1,0:T(8,128)}, f32[304,128]{1,0:T(8,128)S(1)}, u32[]{:S(2)}, u32[]{:S(2)}) collective-permute-start(f32[304,128]{1,0:T(8,128)} %get-tuple-element.45.refs_1_), channel_id=1, source_target_pairs={{0,15},{1,2},{2,1},{3,4},{4,3},{5,6},{6,5},{7,8},{8,7},{9,10},{10,... | collective-permute-start | bytes 466952 | tf_op jit(solution)/shard_map/ppermute | solution.py:44
  10.4 10.7 %collective-permute-start.3 = (f32[96,128]{1,0:T(8,128)}, f32[96,128]{1,0:T(8,128)S(1)}, u32[]{:S(2)}, u32[]{:S(2)}) collective-permute-start(f32[96,128]{1,0:T(8,128)} %get-tuple-element.52), channel_id=1, source_target_pairs={{0,16},{16,0},{1,17},{17,1},{2,18},{18,2},{3,19},{19,3},{4,20},{20... | collective-permute-start | bytes 147464 | tf_op jit(solution)/shard_map/ppermute | solution.py:44
  15.1 11.5 %collective-permute-start.4 = (f32[512,128]{1,0:T(8,128)S(1)}, f32[512,128]{1,0:T(8,128)S(1)}, u32[]{:S(2)}, u32[]{:S(2)}) collective-permute-start(f32[512,128]{1,0:T(8,128)S(1)} %get-tuple-element.54.refs_3_), channel_id=1, source_target_pairs={{0,16},{16,0},{1,17},{17,1},{2,18},{18,2},{3,19},{19,3},{4,20},{20... | collective-permute-start | bytes 786440 | tf_op jit(solution)/shard_map/ppermute | solution.py:44
  16.8 6.3 %collective-permute-start.10 = (f32[56,128]{1,0:T(8,128)S(1)}, f32[56,128]{1,0:T(8,128)S(1)}, u32[]{:S(2)}, u32[]{:S(2)}) collective-permute-start(f32[56,128]{1,0:T(8,128)S(1)} %get-tuple-element.64.refs_1_), channel_id=1, source_target_pairs={{0,8},{1,9},{2,10},{3,11},{4,12},{5,13},{6,14},{7,15},{8,0},{9,1},... | collective-permute-start | bytes 86024 | tf_op jit(solution)/shard_map/ppermute | solution.py:420
  19.4 7.1 %collective-permute-start.5 = (f32[256,128]{1,0:T(8,128)S(1)}, f32[256,128]{1,0:T(8,128)S(1)}, u32[]{:S(2)}, u32[]{:S(2)}) collective-permute-start(f32[256,128]{1,0:T(8,128)S(1)} %get-tuple-element.51.refs_0_.refs_4_), channel_id=1, source_target_pairs={{0,15},{1,2},{2,1},{3,4},{4,3},{5,6},{6,5},{7,8},{8,7},{9,10},{10,... | collective-permute-start | bytes 393224 | tf_op jit(solution)/shard_map/ppermute | solution.py:44
  19.7 6.8 %collective-permute-start.6 = (f32[256,128]{1,0:T(8,128)S(1)}, f32[256,128]{1,0:T(8,128)S(1)}, u32[]{:S(2)}, u32[]{:S(2)}) collective-permute-start(f32[256,128]{1,0:T(8,128)S(1)} %get-tuple-element.55.refs_5_), channel_id=1, source_target_pairs={{0,1},{1,0},{2,3},{3,2},{4,5},{5,4},{6,7},{7,6},{8,9},{9,8},{10,11... | collective-permute-start | bytes 393224 | tf_op jit(solution)/shard_map/ppermute | solution.py:44
  23.1 4.2 %collective-permute-start.11 = (f32[112,128]{1,0:T(8,128)S(1)}, f32[112,128]{1,0:T(8,128)S(1)}, u32[]{:S(2)}, u32[]{:S(2)}) collective-permute-start(f32[112,128]{1,0:T(8,128)S(1)} %shard_map.91.refs_1_), channel_id=1, source_target_pairs={{0,4},{1,5},{2,6},{3,7},{4,0},{5,1},{6,2},{7,3},{8,12},{9,13},{10,... | collective-permute-start | bytes 172040 | tf_op jit(solution)/shard_map/ppermute | solution.py:420
  27.4 4.9 %collective-permute-start.12 = (f32[224,128]{1,0:T(8,128)S(1)}, f32[224,128]{1,0:T(8,128)S(1)}, u32[]{:S(2)}, u32[]{:S(2)}) collective-permute-start(f32[224,128]{1,0:T(8,128)S(1)} %shard_map.92), channel_id=1, source_target_pairs={{0,2},{1,3},{2,0},{3,1},{4,6},{5,7},{6,4},{7,5},{8,10},{9,11},{10,... | collective-permute-start | bytes 344072 | tf_op jit(solution)/shard_map/ppermute | solution.py:420
  29.0 12.7 %collective-permute-start.7 = (f32[896,128]{1,0:T(8,128)S(1)}, f32[896,128]{1,0:T(8,128)S(1)}, u32[]{:S(2)}, u32[]{:S(2)}) collective-permute-start(f32[896,128]{1,0:T(8,128)S(1)} %get-tuple-element.59.refs_0_), channel_id=1, source_target_pairs={{0,16},{16,0},{1,17},{17,1},{2,18},{18,2},{3,19},{19,3},{4,20},{20... | collective-permute-start | bytes 1376264 | tf_op jit(solution)/shard_map/ppermute | solution.py:44
  32.8 8.3 %collective-permute-start.8 = (f32[448,128]{1,0:T(8,128)S(1)}, f32[448,128]{1,0:T(8,128)S(1)}, u32[]{:S(2)}, u32[]{:S(2)}) collective-permute-start(f32[448,128]{1,0:T(8,128)S(1)} %get-tuple-element.61.refs_1_), channel_id=1, source_target_pairs={{0,15},{1,2},{2,1},{3,4},{4,3},{5,6},{6,5},{7,8},{8,7},{9,10},{10,... | collective-permute-start | bytes 688136 | tf_op jit(solution)/shard_map/ppermute | solution.py:44
  36.5 4.9 %collective-permute-start.9 = (f32[448,128]{1,0:T(8,128)S(1)}, f32[448,128]{1,0:T(8,128)S(1)}, u32[]{:S(2)}, u32[]{:S(2)}) collective-permute-start(f32[448,128]{1,0:T(8,128)S(1)} %get-tuple-element.62.refs_2_), channel_id=1, source_target_pairs={{0,1},{1,0},{2,3},{3,2},{4,5},{5,4},{6,7},{7,6},{8,9},{9,8},{10,11... | collective-permute-start | bytes 688136 | tf_op jit(solution)/shard_map/ppermute | solution.py:44
  43.5 8.5 %collective-permute-start.15 = (f32[512,128]{1,0:T(8,128)S(1)}, f32[512,128]{1,0:T(8,128)S(1)}, u32[]{:S(2)}, u32[]{:S(2)}) collective-permute-start(f32[512,128]{1,0:T(8,128)S(1)} %get-tuple-element.67.refs_3_), channel_id=1, source_target_pairs={{0,16},{16,0},{1,17},{17,1},{2,18},{18,2},{3,19},{19,3},{4,20},{20... | collective-permute-start | bytes 786440 | tf_op jit(solution)/shard_map/ppermute | solution.py:44
  44.7 4.7 %collective-permute-start.21 = (f32[24,128]{1,0:T(8,128)S(1)}, f32[24,128]{1,0:T(8,128)S(1)}, u32[]{:S(2)}, u32[]{:S(2)}) collective-permute-start(f32[24,128]{1,0:T(8,128)S(1)} %get-tuple-element.77.refs_1_), channel_id=1, source_target_pairs={{0,8},{1,9},{2,10},{3,11},{4,12},{5,13},{6,14},{7,15},{8,0},{9,1},... | collective-permute-start | bytes 36872 | tf_op jit(solution)/shard_map/ppermute | solution.py:420
  44.8 7.3 %collective-permute-start.16 = (f32[256,128]{1,0:T(8,128)S(1)}, f32[256,128]{1,0:T(8,128)S(1)}, u32[]{:S(2)}, u32[]{:S(2)}) collective-permute-start(f32[256,128]{1,0:T(8,128)S(1)} %get-tuple-element.69.refs_4_.refs_0_), channel_id=1, source_target_pairs={{0,15},{1,2},{2,1},{3,4},{4,3},{5,6},{6,5},{7,8},{8,7},{9,10},{10,... | collective-permute-start | bytes 393224 | tf_op jit(solution)/shard_map/ppermute | solution.py:44
  47.8 4.3 %collective-permute-start.17 = (f32[256,128]{1,0:T(8,128)S(1)}, f32[256,128]{1,0:T(8,128)S(1)}, u32[]{:S(2)}, u32[]{:S(2)}) collective-permute-start(f32[256,128]{1,0:T(8,128)S(1)} %get-tuple-element.70.refs_5_), channel_id=1, source_target_pairs={{0,1},{1,0},{2,3},{3,2},{4,5},{5,4},{6,7},{7,6},{8,9},{9,8},{10,11... | collective-permute-start | bytes 393224 | tf_op jit(solution)/shard_map/ppermute | solution.py:44
  53.2 4.6 %collective-permute-start.23 = (f32[96,128]{1,0:T(8,128)S(1)}, f32[96,128]{1,0:T(8,128)S(1)}, u32[]{:S(2)}, u32[]{:S(2)}) collective-permute-start(f32[96,128]{1,0:T(8,128)S(1)} %shard_map.103), channel_id=1, source_target_pairs={{0,2},{1,3},{2,0},{3,1},{4,6},{5,7},{6,4},{7,5},{8,10},{9,11},{10,... | collective-permute-start | bytes 147464 | tf_op jit(solution)/shard_map/ppermute | solution.py:420
  54.0 9.1 %collective-permute-start.18 = (f32[512,128]{1,0:T(8,128)S(1)}, f32[512,128]{1,0:T(8,128)S(1)}, u32[]{:S(2)}, u32[]{:S(2)}) collective-permute-start(f32[512,128]{1,0:T(8,128)S(1)} %get-tuple-element.72.refs_0_), channel_id=1, source_target_pairs={{0,16},{16,0},{1,17},{17,1},{2,18},{18,2},{3,19},{19,3},{4,20},{20... | collective-permute-start | bytes 786440 | tf_op jit(solution)/shard_map/ppermute | solution.py:44
  55.9 7.2 %collective-permute-start.19 = (f32[256,128]{1,0:T(8,128)S(1)}, f32[256,128]{1,0:T(8,128)S(1)}, u32[]{:S(2)}, u32[]{:S(2)}) collective-permute-start(f32[256,128]{1,0:T(8,128)S(1)} %get-tuple-element.74.refs_1_), channel_id=1, source_target_pairs={{0,15},{1,2},{2,1},{3,4},{4,3},{5,6},{6,5},{7,8},{8,7},{9,10},{10,... | collective-permute-start | bytes 393224 | tf_op jit(solution)/shard_map/ppermute | solution.py:44
  57.8 5.2 %collective-permute-start.20 = (f32[256,128]{1,0:T(8,128)S(1)}, f32[256,128]{1,0:T(8,128)S(1)}, u32[]{:S(2)}, u32[]{:S(2)}) collective-permute-start(f32[256,128]{1,0:T(8,128)S(1)} %get-tuple-element.75.refs_2_), channel_id=1, source_target_pairs={{0,1},{1,0},{2,3},{3,2},{4,5},{5,4},{6,7},{7,6},{8,9},{9,8},{10,11... | collective-permute-start | bytes 393224 | tf_op jit(solution)/shard_map/ppermute | solution.py:44
  64.4 4.7 %collective-permute-start.28 = (f32[24,128]{1,0:T(8,128)S(1)}, f32[24,128]{1,0:T(8,128)S(1)}, u32[]{:S(2)}, u32[]{:S(2)}) collective-permute-start(f32[24,128]{1,0:T(8,128)S(1)} %get-tuple-element.82), channel_id=1, source_target_pairs={{0,8},{1,9},{2,10},{3,11},{4,12},{5,13},{6,14},{7,15},{8,0},{9,1},... | collective-permute-start | bytes 36872 | tf_op jit(solution)/shard_map/ppermute | solution.py:420
  65.0 14.7 %collective-permute-start.32 = (f32[512,128]{1,0:T(8,128)S(1)}, f32[512,128]{1,0:T(8,128)S(1)}, u32[]{:S(2)}, u32[]{:S(2)}) collective-permute-start(f32[512,128]{1,0:T(8,128)S(1)} %shard_map.106.refs_0_.refs_3_), channel_id=1, source_target_pairs={{0,16},{16,0},{1,17},{17,1},{2,18},{18,2},{3,19},{19,3},{4,20},{20... | collective-permute-start | bytes 786440 | tf_op jit(solution)/shard_map/ppermute | solution.py:44
  66.5 10.5 %collective-permute-start.26 = (f32[256,128]{1,0:T(8,128)S(1)}, f32[256,128]{1,0:T(8,128)S(1)}, u32[]{:S(2)}, u32[]{:S(2)}) collective-permute-start(f32[256,128]{1,0:T(8,128)S(1)} %get-tuple-element.80.refs_4_), channel_id=1, source_target_pairs={{0,15},{1,2},{2,1},{3,4},{4,3},{5,6},{6,5},{7,8},{8,7},{9,10},{10,... | collective-permute-start | bytes 393224 | tf_op jit(solution)/shard_map/ppermute | solution.py:44
  68.6 8.5 %collective-permute-start.27 = (f32[256,128]{1,0:T(8,128)S(1)}, f32[256,128]{1,0:T(8,128)S(1)}, u32[]{:S(2)}, u32[]{:S(2)}) collective-permute-start(f32[256,128]{1,0:T(8,128)S(1)} %get-tuple-element.81.refs_5_), channel_id=1, source_target_pairs={{0,1},{1,0},{2,3},{3,2},{4,5},{5,4},{6,7},{7,6},{8,9},{9,8},{10,11... | collective-permute-start | bytes 393224 | tf_op jit(solution)/shard_map/ppermute | solution.py:44
  (21 other events, 105.0 us)
where the time goes:
time: 83.4 us; the launch traced here: 83.3 us
  starting transfers between devices  38.1 us (46%)
  waiting for transfers between devices  25.4 us (30%)
  Pallas kernels  16.4 us (20%)
  local copies, waits for them, and re-layouts  3.03 us (4%)
    ppermute x22, starting transfers between devices, swap(): lax.ppermute(array, axis, [(i, mate(kind, i, devices)) for i in range(dev...  27.6 us
    pallas_call x29, Pallas kernels, call(): pl.pallas_call(lambda *refs: body(*refs[ahead:]), out_shape=outs, in_spec...  16.4 us
    ppermute x22, waiting for transfers between devices, swap(): lax.ppermute(array, axis, [(i, mate(kind, i, devices)) for i in range(dev...  12.7 us
    ppermute x12, waiting for transfers between devices, hop(): return lax.ppermute(piece, 'sub', [(i, i ^ move) for i in range(sub)])  12.7 us
    ppermute x12, starting transfers between devices, hop(): return lax.ppermute(piece, 'sub', [(i, i ^ move) for i in range(sub)])  10.5 us
    unnamed x26, local copies, waits for them, and re-layouts  2.83 us
  transfers between devices with their start and end apart: 34, of which 17 were waited for; matrix products, arithmetic and copies ran while one was open for 0% of the time, Pallas kernels for 12%

commit v1 on v0

--- a/solution.py
+++ b/solution.py
@@ -415,7 +415,7 @@
     return found
 
 
-def gathered(piece, sub, hold=(), wide=False, early=()):
+def gathered(piece, sub, hold=(), wide=False, early=(), done=0):
     def hop(move):
         return lax.ppermute(piece, "sub", [(i, i ^ move) for i in range(sub)])
 
@@ -425,6 +425,8 @@
         pieces = [piece] + [hop(move) for move in (first, second, first ^ second)]
         piece = jnp.concatenate(pieces, axis=0)
     for at, move in enumerate(moves[:-1]):
+        if at < done:
+            continue
         got = hop(move)
         after = hold if at + 1 == len(moves) // 2 else early if at == 0 else ()
         if after:
@@ -494,9 +496,9 @@
     inverse_rows = (rows_of + -rows_of % 8) * tiles
     mapping = None
 
-    def coarse_step(coarse, mapping, hold=(), after=(), early=(), sent=1 + len(near)):
+    def coarse_step(coarse, mapping, hold=(), after=(), early=(), sent=1 + len(near), done=0):
         rows = len(near_order(chans)) * ncl
-        kept, got = gathered(coarse, sub, hold, False, early)
+        kept, got = gathered(coarse, sub, hold, False, early, done)
         if mapping is None:
             mapping, own = call(
                 functools.partial(coarse_first, chans, order, sub, ncl),
@@ -557,12 +559,14 @@
                     (neumann, weights, weighted),
                     flops=flops,
                 )
+                hop = lax.ppermute(coarse, "sub", [(i, i ^ steps(sub)[0]) for i in range(sub)])
+                coarse = call(joining, wide(2 * ncl), (coarse, hop), after=far_scaled[:1])
                 near_scaled = call(
                     functools.partial(smoothing_rows, near),
                     near_plain,
                     (neumann, weights, weighted),
                     flops=flops,
-                    after=far_scaled[:1],
+                    after=(coarse,),
                 )
             else:
                 state, weighted, *far_scaled = call(
@@ -613,7 +617,7 @@
             )
             parts = (*far_parts, *near_parts)
             gots = exchange(chans, parts)
-    mapping, values = coarse_step(coarse, mapping, after=scaled_gots[len(far) :], sent=1)
+    mapping, values = coarse_step(coarse, mapping, hold=near_scaled[:1], after=scaled_gots[: len(far)], sent=1, done=1)
     landed = call(
         functools.partial(landing, chans, ncl),
         wide(iface),

time: 83.4 us -> 83.5 us (level)
  starting transfers between devices: 38.1 us -> 35 us
  waiting for transfers between devices: 25.4 us -> 28.5 us
    ppermute x0 -> x1, waiting for transfers between devices: none -> 4.02 us  [shards(): lax.ppermute(coarse, 'sub', [(i, i ^ steps(sub)[0]) for i in range(sub)])]
    ppermute x12 -> x11, starting transfers between devices: 10.5 us -> 7.5 us  [hop(): return lax.ppermute(piece, 'sub', [(i, i ^ move) for i in range(sub)])]
    ppermute x12 -> x11, waiting for transfers between devices: 12.7 us -> 11.6 us  [hop(): return lax.ppermute(piece, 'sub', [(i, i ^ move) for i in range(sub)])]
    pallas_call x29 -> x31, Pallas kernels: 16.4 us -> 16.4 us  [call(): pl.pallas_call(lambda *refs: body(*refs[ahead:]), out_shape=outs, in_spec...]
    unnamed x26 -> x23, local copies, waits for them, and re-layouts: 2.83 us -> 2.82 us
  transfers between devices with their start and end apart: 34 -> 34, of which waited for: 17 -> 18; matrix products, arithmetic and copies ran while one was open for 0% -> 0% of each run, Pallas kernels for 12% -> 12%
where the time goes in v1:
time: 83.5 us; the launch traced here: 83.3 us
  starting transfers between devices  35 us (42%)
  waiting for transfers between devices  28.5 us (34%)
  Pallas kernels  16.4 us (20%)
  local copies, waits for them, and re-layouts  3.02 us (4%)
    ppermute x22, starting transfers between devices, swap(): lax.ppermute(array, axis, [(i, mate(kind, i, devices)) for i in range(dev...  27.3 us
    pallas_call x31, Pallas kernels, call(): pl.pallas_call(lambda *refs: body(*refs[ahead:]), out_shape=outs, in_spec...  16.4 us
    ppermute x22, waiting for transfers between devices, swap(): lax.ppermute(array, axis, [(i, mate(kind, i, devices)) for i in range(dev...  12.9 us
    ppermute x11, waiting for transfers between devices, hop(): return lax.ppermute(piece, 'sub', [(i, i ^ move) for i in range(sub)])  11.6 us
    ppermute x11, starting transfers between devices, hop(): return lax.ppermute(piece, 'sub', [(i, i ^ move) for i in range(sub)])  7.5 us
    ppermute x1, waiting for transfers between devices, shards(): lax.ppermute(coarse, 'sub', [(i, i ^ steps(sub)[0]) for i in range(sub)])  4.02 us
    unnamed x23, local copies, waits for them, and re-layouts  2.82 us
  transfers between devices with their start and end apart: 34, of which 18 were waited for; matrix products, arithmetic and copies ran while one was open for 0% of the time, Pallas kernels for 12%

profile of v1, /device:TPU:0, one launch (start us, length us, event | category | flops | bytes accessed | tf_op | source)
XLA Modules:
  0.0 83.3 jit_solution(14426696185205088219)
XLA Ops:
  0.0 3.7 %shard_map.82 = (f32[512,128]{1,0:T(8,128)}, f32[304,128]{1,0:T(8,128)}, f32[304,128]{1,0:T(8,128)}, f32[96,128]{1,0:T(8,128)}) custom-call(bf16[1024,1024]{1,0:T(8,128)(2,1)} %bitcast.12, bf16[1024,128]{1,0:T(8,128)(2,1)} %bitcast.24, bf16[1024,128]{1,0:T(8,128)(2,1)} %bitcast.34, bf16[24,1024]{1,0:T(8,128)(2,1)} %bitcast.29), custom_call_target="tpu_custom_call" | custom-call | flops 268435456 | bytes 2670592 | tf_op jit(solution)/shard_map/pallas_call | solution.py:95
  3.7 3.0 %collective-permute-start = (f32[512,128]{1,0:T(8,128)}, f32[512,128]{1,0:T(8,128)S(1)}, u32[]{:S(2)}, u32[]{:S(2)}) collective-permute-start(f32[512,128]{1,0:T(8,128)} %get-tuple-element.44.refs_0_), channel_id=1, source_target_pairs={{0,16},{16,0},{1,17},{17,1},{2,18},{18,2},{3,19},{19,3},{4,20},{20... | collective-permute-start | bytes 786440 | tf_op jit(solution)/shard_map/ppermute | solution.py:44
  6.7 3.7 %collective-permute-start.1 = (f32[304,128]{1,0:T(8,128)}, f32[304,128]{1,0:T(8,128)S(1)}, u32[]{:S(2)}, u32[]{:S(2)}) collective-permute-start(f32[304,128]{1,0:T(8,128)} %get-tuple-element.45.refs_1_), channel_id=1, source_target_pairs={{0,15},{1,2},{2,1},{3,4},{4,3},{5,6},{6,5},{7,8},{8,7},{9,10},{10,... | collective-permute-start | bytes 466952 | tf_op jit(solution)/shard_map/ppermute | solution.py:44
  16.8 2.7 %collective-permute-start.10 = (f32[56,128]{1,0:T(8,128)S(1)}, f32[56,128]{1,0:T(8,128)S(1)}, u32[]{:S(2)}, u32[]{:S(2)}) collective-permute-start(f32[56,128]{1,0:T(8,128)S(1)} %get-tuple-element.64.refs_1_), channel_id=1, source_target_pairs={{0,8},{1,9},{2,10},{3,11},{4,12},{5,13},{6,14},{7,15},{8,0},{9,1},... | collective-permute-start | bytes 86024 | tf_op jit(solution)/shard_map/ppermute | solution.py:420
  19.7 1.4 %collective-permute-start.6 = (f32[256,128]{1,0:T(8,128)S(1)}, f32[256,128]{1,0:T(8,128)S(1)}, u32[]{:S(2)}, u32[]{:S(2)}) collective-permute-start(f32[256,128]{1,0:T(8,128)S(1)} %get-tuple-element.55.refs_5_), channel_id=1, source_target_pairs={{0,1},{1,0},{2,3},{3,2},{4,5},{5,4},{6,7},{7,6},{8,9},{9,8},{10,11... | collective-permute-start | bytes 393224 | tf_op jit(solution)/shard_map/ppermute | solution.py:44
  23.1 1.6 %collective-permute-start.11 = (f32[112,128]{1,0:T(8,128)S(1)}, f32[112,128]{1,0:T(8,128)S(1)}, u32[]{:S(2)}, u32[]{:S(2)}) collective-permute-start(f32[112,128]{1,0:T(8,128)S(1)} %shard_map.91.refs_1_), channel_id=1, source_target_pairs={{0,4},{1,5},{2,6},{3,7},{4,0},{5,1},{6,2},{7,3},{8,12},{9,13},{10,... | collective-permute-start | bytes 172040 | tf_op jit(solution)/shard_map/ppermute | solution.py:420
  24.8 1.8 %collective-permute-done.5.refs_7_ = f32[256,128]{1,0:T(8,128)S(1)} collective-permute-done((f32[256,128]{1,0:T(8,128)S(1)}, f32[256,128]{1,0:T(8,128)S(1)}, u32[]{:S(2)}, u32[]{:S(2)}) %collective-permute-start.5) | collective-permute-done | bytes 131104 | tf_op jit(solution)/shard_map/ppermute | solution.py:44
  27.4 1.6 %collective-permute-start.12 = (f32[224,128]{1,0:T(8,128)S(1)}, f32[224,128]{1,0:T(8,128)S(1)}, u32[]{:S(2)}, u32[]{:S(2)}) collective-permute-start(f32[224,128]{1,0:T(8,128)S(1)} %shard_map.92), channel_id=1, source_target_pairs={{0,2},{1,3},{2,0},{3,1},{4,6},{5,7},{6,4},{7,5},{8,10},{9,11},{10,... | collective-permute-start | bytes 344072 | tf_op jit(solution)/shard_map/ppermute | solution.py:420
  29.5 2.7 %collective-permute-done.12 = f32[224,128]{1,0:T(8,128)S(1)} collective-permute-done((f32[224,128]{1,0:T(8,128)S(1)}, f32[224,128]{1,0:T(8,128)S(1)}, u32[]{:S(2)}, u32[]{:S(2)}) %collective-permute-start.12) | collective-permute-done | bytes 114720 | tf_op jit(solution)/shard_map/ppermute | solution.py:420
  32.8 3.7 %collective-permute-start.8 = (f32[448,128]{1,0:T(8,128)S(1)}, f32[448,128]{1,0:T(8,128)S(1)}, u32[]{:S(2)}, u32[]{:S(2)}) collective-permute-start(f32[448,128]{1,0:T(8,128)S(1)} %get-tuple-element.61.refs_1_), channel_id=1, source_target_pairs={{0,15},{1,2},{2,1},{3,4},{4,3},{5,6},{6,5},{7,8},{8,7},{9,10},{10,... | collective-permute-start | bytes 688136 | tf_op jit(solution)/shard_map/ppermute | solution.py:44
  36.5 1.9 %shard_map.93 = (bf16[120,1152]{1,0:T(8,128)(2,1)S(1)}, f32[120,128]{1,0:T(8,128)S(1)}) custom-call(s32[1,384]{1,0:T(1,128)S(1)} %copy-done.8, f32[448,128]{1,0:T(8,128)S(1)} %pad_maximum_fusion.refs_1_, f32[448,128]{1,0:T(8,128)S(1)} %collective-permute-done.13.refs_2_), custom_call_target="tpu_custom_call" | custom-call | bytes 460288 | tf_op jit(solution)/shard_map/pallas_call | solution.py:95
  39.1 2.0 %collective-permute-done.8.refs_4_.refs_2_ = f32[448,128]{1,0:T(8,128)S(1)} collective-permute-done((f32[448,128]{1,0:T(8,128)S(1)}, f32[448,128]{1,0:T(8,128)S(1)}, u32[]{:S(2)}, u32[]{:S(2)}) %collective-permute-start.8) | collective-permute-done | bytes 229408 | tf_op jit(solution)/shard_map/ppermute | solution.py:44
  44.8 3.0 %collective-permute-start.16 = (f32[256,128]{1,0:T(8,128)S(1)}, f32[256,128]{1,0:T(8,128)S(1)}, u32[]{:S(2)}, u32[]{:S(2)}) collective-permute-start(f32[256,128]{1,0:T(8,128)S(1)} %get-tuple-element.69.refs_4_.refs_0_), channel_id=1, source_target_pairs={{0,15},{1,2},{2,1},{3,4},{4,3},{5,6},{6,5},{7,8},{8,7},{9,10},{10,... | collective-permute-start | bytes 393224 | tf_op jit(solution)/shard_map/ppermute | solution.py:44
  47.8 1.6 %collective-permute-done.21.refs_2_ = f32[24,128]{1,0:T(8,128)S(1)} collective-permute-done((f32[24,128]{1,0:T(8,128)S(1)}, f32[24,128]{1,0:T(8,128)S(1)}, u32[]{:S(2)}, u32[]{:S(2)}) %collective-permute-start.21) | collective-permute-done | bytes 12320 | tf_op jit(solution)/shard_map/ppermute | solution.py:420
  49.4 2.6 %collective-permute-done.16.refs_7_ = f32[256,128]{1,0:T(8,128)S(1)} collective-permute-done((f32[256,128]{1,0:T(8,128)S(1)}, f32[256,128]{1,0:T(8,128)S(1)}, u32[]{:S(2)}, u32[]{:S(2)}) %collective-permute-start.16) | collective-permute-done | bytes 131104 | tf_op jit(solution)/shard_map/ppermute | solution.py:44
  54.0 1.5 %collective-permute-start.18 = (f32[512,128]{1,0:T(8,128)S(1)}, f32[512,128]{1,0:T(8,128)S(1)}, u32[]{:S(2)}, u32[]{:S(2)}) collective-permute-start(f32[512,128]{1,0:T(8,128)S(1)} %get-tuple-element.72.refs_0_), channel_id=1, source_target_pairs={{0,16},{16,0},{1,17},{17,1},{2,18},{18,2},{3,19},{19,3},{4,20},{20... | collective-permute-start | bytes 786440 | tf_op jit(solution)/shard_map/ppermute | solution.py:44
  55.9 1.9 %collective-permute-start.19 = (f32[256,128]{1,0:T(8,128)S(1)}, f32[256,128]{1,0:T(8,128)S(1)}, u32[]{:S(2)}, u32[]{:S(2)}) collective-permute-start(f32[256,128]{1,0:T(8,128)S(1)} %get-tuple-element.74.refs_1_), channel_id=1, source_target_pairs={{0,15},{1,2},{2,1},{3,4},{4,3},{5,6},{6,5},{7,8},{8,7},{9,10},{10,... | collective-permute-start | bytes 393224 | tf_op jit(solution)/shard_map/ppermute | solution.py:44
  60.5 2.5 %collective-permute-done.19.refs_4_ = f32[256,128]{1,0:T(8,128)S(1)} collective-permute-done((f32[256,128]{1,0:T(8,128)S(1)}, f32[256,128]{1,0:T(8,128)S(1)}, u32[]{:S(2)}, u32[]{:S(2)}) %collective-permute-start.19) | collective-permute-done | bytes 131104 | tf_op jit(solution)/shard_map/ppermute | solution.py:44
  65.0 4.0 %collective-permute-done.27.refs_2_ = f32[24,128]{1,0:T(8,128)S(1)} collective-permute-done((f32[24,128]{1,0:T(8,128)S(1)}, f32[24,128]{1,0:T(8,128)S(1)}, u32[]{:S(2)}, u32[]{:S(2)}) %collective-permute-start.27) | collective-permute-done | bytes 12320 | tf_op jit(solution)/shard_map/ppermute | solution.py:562
  70.7 2.1 %collective-permute-done.28.refs_2_ = f32[48,128]{1,0:T(8,128)S(1)} collective-permute-done((f32[48,128]{1,0:T(8,128)S(1)}, f32[48,128]{1,0:T(8,128)S(1)}, u32[]{:S(2)}, u32[]{:S(2)}) %collective-permute-start.28) | collective-permute-done | bytes 24608 | tf_op jit(solution)/shard_map/ppermute | solution.py:420
  73.0 2.1 %collective-permute-start.32 = (f32[256,128]{1,0:T(8,128)S(1)}, f32[256,128]{1,0:T(8,128)S(1)}, u32[]{:S(2)}, u32[]{:S(2)}) collective-permute-start(f32[256,128]{1,0:T(8,128)S(1)} %get-tuple-element.82.refs_5_), channel_id=1, source_target_pairs={{0,1},{1,0},{2,3},{3,2},{4,5},{5,4},{6,7},{7,6},{8,9},{9,8},{10,11... | collective-permute-start | bytes 393224 | tf_op jit(solution)/shard_map/ppermute | solution.py:44
  75.0 1.9 %collective-permute-done.29 = f32[96,128]{1,0:T(8,128)S(1)} collective-permute-done((f32[96,128]{1,0:T(8,128)S(1)}, f32[96,128]{1,0:T(8,128)S(1)}, u32[]{:S(2)}, u32[]{:S(2)}) %collective-permute-start.29) | collective-permute-done | bytes 49184 | tf_op jit(solution)/shard_map/ppermute | solution.py:420
  77.1 1.3 %collective-permute-done.30.refs_3_ = f32[192,128]{1,0:T(8,128)S(1)} collective-permute-done((f32[192,128]{1,0:T(8,128)S(1)}, f32[192,128]{1,0:T(8,128)S(1)}, u32[]{:S(2)}, u32[]{:S(2)}) %collective-permute-start.30) | collective-permute-done | bytes 98336 | tf_op jit(solution)/shard_map/ppermute | solution.py:420
  80.4 2.1 %collective-permute-done.33.refs_3_ = f32[24,128]{1,0:T(8,128)S(1)} collective-permute-done((f32[24,128]{1,0:T(8,128)S(1)}, f32[24,128]{1,0:T(8,128)S(1)}, u32[]{:S(2)}, u32[]{:S(2)}) %collective-permute-start.33) | collective-permute-done | bytes 12320 | tf_op jit(solution)/shard_map/ppermute | solution.py:44
  (105 shorter events, 26.5 us)
Async XLA Ops:
  3.7 10.6 %collective-permute-start = (f32[512,128]{1,0:T(8,128)}, f32[512,128]{1,0:T(8,128)S(1)}, u32[]{:S(2)}, u32[]{:S(2)}) collective-permute-start(f32[512,128]{1,0:T(8,128)} %get-tuple-element.44.refs_0_), channel_id=1, source_target_pairs={{0,16},{16,0},{1,17},{17,1},{2,18},{18,2},{3,19},{19,3},{4,20},{20... | collective-permute-start | bytes 786440 | tf_op jit(solution)/shard_map/ppermute | solution.py:44
  6.7 7.6 %collective-permute-start.1 = (f32[304,128]{1,0:T(8,128)}, f32[304,128]{1,0:T(8,128)S(1)}, u32[]{:S(2)}, u32[]{:S(2)}) collective-permute-start(f32[304,128]{1,0:T(8,128)} %get-tuple-element.45.refs_1_), channel_id=1, source_target_pairs={{0,15},{1,2},{2,1},{3,4},{4,3},{5,6},{6,5},{7,8},{8,7},{9,10},{10,... | collective-permute-start | bytes 466952 | tf_op jit(solution)/shard_map/ppermute | solution.py:44
  10.4 10.7 %collective-permute-start.3 = (f32[96,128]{1,0:T(8,128)}, f32[96,128]{1,0:T(8,128)S(1)}, u32[]{:S(2)}, u32[]{:S(2)}) collective-permute-start(f32[96,128]{1,0:T(8,128)} %get-tuple-element.52), channel_id=1, source_target_pairs={{0,16},{16,0},{1,17},{17,1},{2,18},{18,2},{3,19},{19,3},{4,20},{20... | collective-permute-start | bytes 147464 | tf_op jit(solution)/shard_map/ppermute | solution.py:44
  15.1 11.5 %collective-permute-start.4 = (f32[512,128]{1,0:T(8,128)S(1)}, f32[512,128]{1,0:T(8,128)S(1)}, u32[]{:S(2)}, u32[]{:S(2)}) collective-permute-start(f32[512,128]{1,0:T(8,128)S(1)} %get-tuple-element.54.refs_3_), channel_id=1, source_target_pairs={{0,16},{16,0},{1,17},{17,1},{2,18},{18,2},{3,19},{19,3},{4,20},{20... | collective-permute-start | bytes 786440 | tf_op jit(solution)/shard_map/ppermute | solution.py:44
  16.8 6.3 %collective-permute-start.10 = (f32[56,128]{1,0:T(8,128)S(1)}, f32[56,128]{1,0:T(8,128)S(1)}, u32[]{:S(2)}, u32[]{:S(2)}) collective-permute-start(f32[56,128]{1,0:T(8,128)S(1)} %get-tuple-element.64.refs_1_), channel_id=1, source_target_pairs={{0,8},{1,9},{2,10},{3,11},{4,12},{5,13},{6,14},{7,15},{8,0},{9,1},... | collective-permute-start | bytes 86024 | tf_op jit(solution)/shard_map/ppermute | solution.py:420
  19.4 7.1 %collective-permute-start.5 = (f32[256,128]{1,0:T(8,128)S(1)}, f32[256,128]{1,0:T(8,128)S(1)}, u32[]{:S(2)}, u32[]{:S(2)}) collective-permute-start(f32[256,128]{1,0:T(8,128)S(1)} %get-tuple-element.51.refs_0_.refs_4_), channel_id=1, source_target_pairs={{0,15},{1,2},{2,1},{3,4},{4,3},{5,6},{6,5},{7,8},{8,7},{9,10},{10,... | collective-permute-start | bytes 393224 | tf_op jit(solution)/shard_map/ppermute | solution.py:44
  19.7 6.8 %collective-permute-start.6 = (f32[256,128]{1,0:T(8,128)S(1)}, f32[256,128]{1,0:T(8,128)S(1)}, u32[]{:S(2)}, u32[]{:S(2)}) collective-permute-start(f32[256,128]{1,0:T(8,128)S(1)} %get-tuple-element.55.refs_5_), channel_id=1, source_target_pairs={{0,1},{1,0},{2,3},{3,2},{4,5},{5,4},{6,7},{7,6},{8,9},{9,8},{10,11... | collective-permute-start | bytes 393224 | tf_op jit(solution)/shard_map/ppermute | solution.py:44
  23.1 4.2 %collective-permute-start.11 = (f32[112,128]{1,0:T(8,128)S(1)}, f32[112,128]{1,0:T(8,128)S(1)}, u32[]{:S(2)}, u32[]{:S(2)}) collective-permute-start(f32[112,128]{1,0:T(8,128)S(1)} %shard_map.91.refs_1_), channel_id=1, source_target_pairs={{0,4},{1,5},{2,6},{3,7},{4,0},{5,1},{6,2},{7,3},{8,12},{9,13},{10,... | collective-permute-start | bytes 172040 | tf_op jit(solution)/shard_map/ppermute | solution.py:420
  27.4 4.9 %collective-permute-start.12 = (f32[224,128]{1,0:T(8,128)S(1)}, f32[224,128]{1,0:T(8,128)S(1)}, u32[]{:S(2)}, u32[]{:S(2)}) collective-permute-start(f32[224,128]{1,0:T(8,128)S(1)} %shard_map.92), channel_id=1, source_target_pairs={{0,2},{1,3},{2,0},{3,1},{4,6},{5,7},{6,4},{7,5},{8,10},{9,11},{10,... | collective-permute-start | bytes 344072 | tf_op jit(solution)/shard_map/ppermute | solution.py:420
  29.0 12.7 %collective-permute-start.7 = (f32[896,128]{1,0:T(8,128)S(1)}, f32[896,128]{1,0:T(8,128)S(1)}, u32[]{:S(2)}, u32[]{:S(2)}) collective-permute-start(f32[896,128]{1,0:T(8,128)S(1)} %get-tuple-element.59.refs_0_), channel_id=1, source_target_pairs={{0,16},{16,0},{1,17},{17,1},{2,18},{18,2},{3,19},{19,3},{4,20},{20... | collective-permute-start | bytes 1376264 | tf_op jit(solution)/shard_map/ppermute | solution.py:44
  32.8 8.3 %collective-permute-start.8 = (f32[448,128]{1,0:T(8,128)S(1)}, f32[448,128]{1,0:T(8,128)S(1)}, u32[]{:S(2)}, u32[]{:S(2)}) collective-permute-start(f32[448,128]{1,0:T(8,128)S(1)} %get-tuple-element.61.refs_1_), channel_id=1, source_target_pairs={{0,15},{1,2},{2,1},{3,4},{4,3},{5,6},{6,5},{7,8},{8,7},{9,10},{10,... | collective-permute-start | bytes 688136 | tf_op jit(solution)/shard_map/ppermute | solution.py:44
  36.5 4.9 %collective-permute-start.9 = (f32[448,128]{1,0:T(8,128)S(1)}, f32[448,128]{1,0:T(8,128)S(1)}, u32[]{:S(2)}, u32[]{:S(2)}) collective-permute-start(f32[448,128]{1,0:T(8,128)S(1)} %get-tuple-element.62.refs_2_), channel_id=1, source_target_pairs={{0,1},{1,0},{2,3},{3,2},{4,5},{5,4},{6,7},{7,6},{8,9},{9,8},{10,11... | collective-permute-start | bytes 688136 | tf_op jit(solution)/shard_map/ppermute | solution.py:44
  43.5 8.5 %collective-permute-start.15 = (f32[512,128]{1,0:T(8,128)S(1)}, f32[512,128]{1,0:T(8,128)S(1)}, u32[]{:S(2)}, u32[]{:S(2)}) collective-permute-start(f32[512,128]{1,0:T(8,128)S(1)} %get-tuple-element.67.refs_3_), channel_id=1, source_target_pairs={{0,16},{16,0},{1,17},{17,1},{2,18},{18,2},{3,19},{19,3},{4,20},{20... | collective-permute-start | bytes 786440 | tf_op jit(solution)/shard_map/ppermute | solution.py:44
  44.7 4.7 %collective-permute-start.21 = (f32[24,128]{1,0:T(8,128)S(1)}, f32[24,128]{1,0:T(8,128)S(1)}, u32[]{:S(2)}, u32[]{:S(2)}) collective-permute-start(f32[24,128]{1,0:T(8,128)S(1)} %get-tuple-element.77.refs_1_), channel_id=1, source_target_pairs={{0,8},{1,9},{2,10},{3,11},{4,12},{5,13},{6,14},{7,15},{8,0},{9,1},... | collective-permute-start | bytes 36872 | tf_op jit(solution)/shard_map/ppermute | solution.py:420
  44.8 7.3 %collective-permute-start.16 = (f32[256,128]{1,0:T(8,128)S(1)}, f32[256,128]{1,0:T(8,128)S(1)}, u32[]{:S(2)}, u32[]{:S(2)}) collective-permute-start(f32[256,128]{1,0:T(8,128)S(1)} %get-tuple-element.69.refs_4_.refs_0_), channel_id=1, source_target_pairs={{0,15},{1,2},{2,1},{3,4},{4,3},{5,6},{6,5},{7,8},{8,7},{9,10},{10,... | collective-permute-start | bytes 393224 | tf_op jit(solution)/shard_map/ppermute | solution.py:44
  47.8 4.3 %collective-permute-start.17 = (f32[256,128]{1,0:T(8,128)S(1)}, f32[256,128]{1,0:T(8,128)S(1)}, u32[]{:S(2)}, u32[]{:S(2)}) collective-permute-start(f32[256,128]{1,0:T(8,128)S(1)} %get-tuple-element.70.refs_5_), channel_id=1, source_target_pairs={{0,1},{1,0},{2,3},{3,2},{4,5},{5,4},{6,7},{7,6},{8,9},{9,8},{10,11... | collective-permute-start | bytes 393224 | tf_op jit(solution)/shard_map/ppermute | solution.py:44
  53.2 4.6 %collective-permute-start.23 = (f32[96,128]{1,0:T(8,128)S(1)}, f32[96,128]{1,0:T(8,128)S(1)}, u32[]{:S(2)}, u32[]{:S(2)}) collective-permute-start(f32[96,128]{1,0:T(8,128)S(1)} %shard_map.103), channel_id=1, source_target_pairs={{0,2},{1,3},{2,0},{3,1},{4,6},{5,7},{6,4},{7,5},{8,10},{9,11},{10,... | collective-permute-start | bytes 147464 | tf_op jit(solution)/shard_map/ppermute | solution.py:420
  54.0 9.1 %collective-permute-start.18 = (f32[512,128]{1,0:T(8,128)S(1)}, f32[512,128]{1,0:T(8,128)S(1)}, u32[]{:S(2)}, u32[]{:S(2)}) collective-permute-start(f32[512,128]{1,0:T(8,128)S(1)} %get-tuple-element.72.refs_0_), channel_id=1, source_target_pairs={{0,16},{16,0},{1,17},{17,1},{2,18},{18,2},{3,19},{19,3},{4,20},{20... | collective-permute-start | bytes 786440 | tf_op jit(solution)/shard_map/ppermute | solution.py:44
  55.9 7.2 %collective-permute-start.19 = (f32[256,128]{1,0:T(8,128)S(1)}, f32[256,128]{1,0:T(8,128)S(1)}, u32[]{:S(2)}, u32[]{:S(2)}) collective-permute-start(f32[256,128]{1,0:T(8,128)S(1)} %get-tuple-element.74.refs_1_), channel_id=1, source_target_pairs={{0,15},{1,2},{2,1},{3,4},{4,3},{5,6},{6,5},{7,8},{8,7},{9,10},{10,... | collective-permute-start | bytes 393224 | tf_op jit(solution)/shard_map/ppermute | solution.py:44
  57.8 5.2 %collective-permute-start.20 = (f32[256,128]{1,0:T(8,128)S(1)}, f32[256,128]{1,0:T(8,128)S(1)}, u32[]{:S(2)}, u32[]{:S(2)}) collective-permute-start(f32[256,128]{1,0:T(8,128)S(1)} %get-tuple-element.75.refs_2_), channel_id=1, source_target_pairs={{0,1},{1,0},{2,3},{3,2},{4,5},{5,4},{6,7},{7,6},{8,9},{9,8},{10,11... | collective-permute-start | bytes 393224 | tf_op jit(solution)/shard_map/ppermute | solution.py:44
  64.4 4.7 %collective-permute-start.27 = (f32[24,128]{1,0:T(8,128)S(1)}, f32[24,128]{1,0:T(8,128)S(1)}, u32[]{:S(2)}, u32[]{:S(2)}) collective-permute-start(f32[24,128]{1,0:T(8,128)S(1)} %get-tuple-element.80.refs_1_), channel_id=1, source_target_pairs={{0,8},{1,9},{2,10},{3,11},{4,12},{5,13},{6,14},{7,15},{8,0},{9,1},... | collective-permute-start | bytes 36872 | tf_op jit(solution)/shard_map/ppermute | solution.py:562
  69.1 9.3 %collective-permute-start.26 = (f32[512,128]{1,0:T(8,128)S(1)}, f32[512,128]{1,0:T(8,128)S(1)}, u32[]{:S(2)}, u32[]{:S(2)}) collective-permute-start(f32[512,128]{1,0:T(8,128)S(1)} %shard_map.106.refs_0_.refs_3_), channel_id=1, source_target_pairs={{0,16},{16,0},{1,17},{17,1},{2,18},{18,2},{3,19},{19,3},{4,20},{20... | collective-permute-start | bytes 786440 | tf_op jit(solution)/shard_map/ppermute | solution.py:44
  73.0 7.1 %collective-permute-start.31 = (f32[256,128]{1,0:T(8,128)S(1)}, f32[256,128]{1,0:T(8,128)S(1)}, u32[]{:S(2)}, u32[]{:S(2)}) collective-permute-start(f32[256,128]{1,0:T(8,128)S(1)} %get-tuple-element.81.refs_0_.refs_4_), channel_id=1, source_target_pairs={{0,15},{1,2},{2,1},{3,4},{4,3},{5,6},{6,5},{7,8},{8,7},{9,10},{10,... | collective-permute-start | bytes 393224 | tf_op jit(solution)/shard_map/ppermute | solution.py:44
  73.0 7.1 %collective-permute-start.32 = (f32[256,128]{1,0:T(8,128)S(1)}, f32[256,128]{1,0:T(8,128)S(1)}, u32[]{:S(2)}, u32[]{:S(2)}) collective-permute-start(f32[256,128]{1,0:T(8,128)S(1)} %get-tuple-element.82.refs_5_), channel_id=1, source_target_pairs={{0,1},{1,0},{2,3},{3,2},{4,5},{5,4},{6,7},{7,6},{8,9},{9,8},{10,11... | collective-permute-start | bytes 393224 | tf_op jit(solution)/shard_map/ppermute | solution.py:44
  (21 other events, 105.1 us)
